TPU v7x, 32 devices: a whole 2x2x4 slice. The times are simulated.
32 devices in a mesh: ctx: 4 (over z), exp: 8 (over y, x, core).
Axes of the slice: x: 2, y: 2, z: 4, core: 2. Of those that a mesh axis runs over, the one named last changes fastest.
Arguments:
- tokens_in: bfloat16 [16, 1024, 768], P('exp', 'ctx'), may hold values from -6 to 6
- first_gain: bfloat16 [768], P('exp'), may hold values from 0.099609375 to 1.8984375
- joint_projection: bfloat16 [768, 2304], P('exp'), may hold values from -0.21875 to 0.21875
- out_projection: bfloat16 [768, 768], P('exp'), may hold values from -2.5 to 2.5
- bias_table: bfloat16 [32, 12], P('exp'), may hold values from -4 to 4
- second_gain: bfloat16 [768], P('exp'), may hold values from 0.099609375 to 1.8984375
- router_weight: bfloat16 [768, 8], P('exp'), may hold values from -0.15625 to 0.15625
- expert_up: bfloat16 [8, 768, 3072], P('exp', None, 'ctx'), may hold values from -0.21875 to 0.21875
- expert_down: bfloat16 [8, 3072, 768], P('exp', 'ctx'), may hold values from -0.95703125 to 0.95703125
- expert_index: int32 [16, 1024, 1], P('exp', 'ctx'), may hold values from 0 to 7; in each aligned block of 256 rows (0 to 255, 256 to 511, ..., all dimensions but the last counted through in order) at most 40 rows name the same one
- keep_mask: int32 [16, 1024], P('exp', 'ctx'), may hold values 0 or 1
- buckets: int32 [2047], replicated, may hold values from 0 to 31
- cotangent: bfloat16 [16, 1024, 768], P('exp', 'ctx'), may hold values from -6 to 6
Outputs:
- layer_out: bfloat16 [16, 1024, 768], P('exp', 'ctx')
- grad_tokens: float32 [16, 1024, 768], P('exp', 'ctx')
- grad_first_gain: float32 [768], P('exp')
- grad_joint: float32 [768, 2304], P('exp')
- grad_out_projection: float32 [768, 768], P('exp')
- grad_bias_table: float32 [32, 12], P('exp')
- grad_second_gain: float32 [768], P('exp')
- grad_router: float32 [768, 8], P('exp')
- grad_expert_up: float32 [8, 768, 3072], P('exp', None, 'ctx')
- grad_expert_down: float32 [8, 3072, 768], P('exp', 'ctx')
Inputs may be any that keep to these rules, and one draw needn't show every extreme that they name: `expert_index`: within each aligned block of 256 positions of a sequence, no expert is named by more than 40 tokens.
All inputs are finite; a program needn't handle non-finite values. No bound on the sum of `keep_mask` on one device may be relied on, other than what follows from the above.
Results may differ from a plain program's by a relative error of at most 0.02.
Values may be sent and summed in bfloat16 or wider, within the bound.
No kernel may reach another device: no remote copies, remote signals or barrier semaphores. Data moves between devices by JAX's collectives and lax.ppermute only.
A program may use at most 256 MiB of HBM per device.

v0:
```python
import math

import jax
import jax.numpy as jnp
from jax import lax
from jax.sharding import PartitionSpec as P

EPSILON = 1e-06
SCORE_SCALE = 0.125
HIGHEST = lax.Precision.HIGHEST


def rms_forward(row_data, gain_vec):
    inverse = lax.rsqrt(jnp.mean(row_data * row_data, axis=-1, keepdims=True) + EPSILON)
    return (row_data * inverse * gain_vec, inverse)


def rms_backward(row_data, inverse, gain_vec, grad_out):
    normed = row_data * inverse
    grad_gain = jnp.sum(grad_out * normed, axis=(0, 1))
    scaled = grad_out * gain_vec
    spread = jnp.mean(scaled * normed, axis=-1, keepdims=True)
    return (inverse * (scaled - normed * spread), grad_gain)


def bias_block(offset_values, base_offset, row_count, col_count):
    span = row_count + col_count - 1
    window = lax.dynamic_slice_in_dim(offset_values, base_offset, span, 1)
    head_count = window.shape[0]
    tiled = jnp.broadcast_to(window[:, None, :], (head_count, row_count, span)).reshape(
        head_count, row_count * span
    )
    skewed = tiled[:, row_count - 1 : row_count - 1 + row_count * (span - 1)].reshape(
        head_count, row_count, span - 1
    )
    return skewed[:, :, :col_count]


def add_offsets(grad_off, grad_scores, base_offset):
    sums = jnp.sum(grad_scores.astype(jnp.float32), axis=0)
    head_count, row_count, col_count = sums.shape
    span = row_count + col_count - 1
    widened = jnp.pad(sums, ((0, 0), (0, 0), (0, span - 1 - col_count))).reshape(
        head_count, row_count * (span - 1)
    )
    placed = jnp.pad(widened, ((0, 0), (row_count - 1, 1))).reshape(head_count, row_count, span)
    window = jnp.sum(placed, axis=1)
    current = lax.dynamic_slice_in_dim(grad_off, base_offset, span, 1)
    return lax.dynamic_update_slice_in_dim(grad_off, current + window, base_offset, 1)


def block_scores(queries, key_rows, bias_grid):
    raw_scores = jnp.einsum(
        "srhe,sche->shrc", queries, key_rows, preferred_element_type=jnp.float32
    )
    return raw_scores * SCORE_SCALE + bias_grid[None]


def key_reader(gathered, offset_values, ctx_place, block_len, head_count, head_size):
    seq_count, seq_len, double_width = gathered.shape
    model_width = double_width // 2
    key_block = math.gcd(512, seq_len)

    def keys_at(block_index):
        block_start = block_index * key_block
        key_piece = lax.dynamic_slice_in_dim(gathered, block_start, key_block, 1)
        key_rows = key_piece[..., :model_width].reshape(seq_count, key_block, head_count, head_size)
        value_rows = key_piece[..., model_width:].reshape(
            seq_count, key_block, head_count, head_size
        )
        base_offset = block_start - ctx_place * block_len + seq_len - block_len
        return (
            key_rows,
            value_rows,
            bias_block(offset_values, base_offset, block_len, key_block),
            base_offset,
            block_start,
        )

    return (keys_at, seq_len // key_block, key_block)


def attend_forward(queries, gathered, offset_values, ctx_place):
    seq_count, block_len, head_count, head_size = queries.shape
    keys_at, block_count, key_block = key_reader(
        gathered, offset_values, ctx_place, block_len, head_count, head_size
    )

    def stats_step(block_index, state_now):
        row_top, row_total = state_now
        key_rows, value_rows, bias_grid, base_offset, block_start = keys_at(block_index)
        scores = block_scores(queries, key_rows, bias_grid)
        new_top = jnp.maximum(row_top, jnp.max(scores, axis=-1))
        row_total = row_total * jnp.exp(row_top - new_top) + jnp.sum(
            jnp.exp(scores - new_top[..., None]), axis=-1
        )
        return (new_top, row_total)

    init_top = jnp.full((seq_count, head_count, block_len), -jnp.inf, jnp.float32)
    init_total = jnp.zeros((seq_count, head_count, block_len), jnp.float32)
    row_top, row_total = lax.fori_loop(0, block_count, stats_step, (init_top, init_total))
    logsum = row_top + jnp.log(row_total)

    def value_step(block_index, accum):
        key_rows, value_rows, bias_grid, base_offset, block_start = keys_at(block_index)
        weights = jnp.exp(block_scores(queries, key_rows, bias_grid) - logsum[..., None]).astype(
            jnp.bfloat16
        )
        return accum + jnp.einsum(
            "shrc,sche->srhe", weights, value_rows, preferred_element_type=jnp.float32
        )

    outputs = lax.fori_loop(
        0,
        block_count,
        value_step,
        jnp.zeros((seq_count, block_len, head_count, head_size), jnp.float32),
    )
    return (outputs, logsum)


def attend_backward(queries, grad_heads, gathered, offset_values, logsum, row_delta, ctx_place):
    seq_count, block_len, head_count, head_size = queries.shape
    model_width = head_count * head_size
    keys_at, block_count, key_block = key_reader(
        gathered, offset_values, ctx_place, block_len, head_count, head_size
    )
    seq_len = gathered.shape[1]

    def back_step(block_index, state_now):
        grad_q, grad_off, grad_kv = state_now
        key_rows, value_rows, bias_grid, base_offset, block_start = keys_at(block_index)
        weights = jnp.exp(block_scores(queries, key_rows, bias_grid) - logsum[..., None])
        grad_p = jnp.einsum(
            "srhe,sche->shrc", grad_heads, value_rows, preferred_element_type=jnp.float32
        )
        grad_scores = (weights * (grad_p - row_delta[..., None])).astype(jnp.bfloat16)
        grad_q = grad_q + jnp.einsum(
            "shrc,sche->srhe", grad_scores, key_rows, preferred_element_type=jnp.float32
        )
        grad_off = add_offsets(grad_off, grad_scores, base_offset)
        grad_k = (
            jnp.einsum("shrc,srhe->sche", grad_scores, queries, preferred_element_type=jnp.float32)
            * SCORE_SCALE
        )
        grad_v = jnp.einsum(
            "shrc,srhe->sche",
            weights.astype(jnp.bfloat16),
            grad_heads,
            preferred_element_type=jnp.float32,
        )
        key_piece = jnp.concatenate(
            [
                grad_k.reshape(seq_count, key_block, model_width),
                grad_v.reshape(seq_count, key_block, model_width),
            ],
            axis=-1,
        )
        grad_kv = lax.dynamic_update_slice_in_dim(grad_kv, key_piece, block_start, 1)
        return (grad_q, grad_off, grad_kv)

    init_q = jnp.zeros((seq_count, block_len, head_count, head_size), jnp.float32)
    init_off = jnp.zeros(offset_values.shape, jnp.float32)
    init_kv = jnp.zeros((seq_count, seq_len, 2 * model_width), jnp.float32)
    grad_q, grad_off, grad_kv = lax.fori_loop(
        0, block_count, back_step, (init_q, init_off, init_kv)
    )
    return (grad_q * SCORE_SCALE, grad_off, grad_kv)


def per_device(
    tokens_in,
    first_gain,
    joint_projection,
    out_projection,
    bias_table,
    second_gain,
    router_weight,
    expert_up,
    expert_down,
    expert_index,
    keep_mask,
    buckets,
    cotangent,
):
    gain_one, weight_joint, weight_out, table, gain_two, weight_router = (
        lax.all_gather(first_gain, "exp", axis=0, tiled=True),
        lax.all_gather(joint_projection, "exp", axis=0, tiled=True),
        lax.all_gather(out_projection, "exp", axis=0, tiled=True),
        lax.all_gather(bias_table, "exp", axis=0, tiled=True),
        lax.all_gather(second_gain, "exp", axis=0, tiled=True),
        lax.all_gather(router_weight, "exp", axis=0, tiled=True),
    )
    weight_up, weight_down = (
        lax.all_gather(expert_up, "ctx", axis=2, tiled=True),
        lax.all_gather(expert_down, "ctx", axis=1, tiled=True),
    )
    seq_count, block_len, model_width = tokens_in.shape
    head_count = table.shape[1]
    head_size = model_width // head_count
    ctx_place = lax.axis_index("ctx")
    tokens_f = tokens_in.astype(jnp.float32)
    gain_first = gain_one.astype(jnp.float32)
    gain_second = gain_two.astype(jnp.float32)
    normed_one, inverse_one = rms_forward(tokens_f, gain_first)
    hidden_one = normed_one.astype(jnp.bfloat16)
    projected = jnp.dot(hidden_one, weight_joint, preferred_element_type=jnp.float32).astype(
        jnp.bfloat16
    )
    queries = projected[..., :model_width].reshape(seq_count, block_len, head_count, head_size)
    key_values = projected[..., model_width:]
    gathered = lax.all_gather(key_values, "ctx", axis=1, tiled=True)
    bucket_hot = (buckets[None, :] == jnp.arange(table.shape[0], dtype=jnp.int32)[:, None]).astype(
        jnp.float32
    )
    offset_values = jnp.dot(table.astype(jnp.float32).T, bucket_hot, precision=HIGHEST)
    attended, logsum = attend_forward(queries, gathered, offset_values, ctx_place)
    attended_low = attended.reshape(seq_count, block_len, model_width).astype(jnp.bfloat16)
    residual = tokens_f + jnp.dot(attended_low, weight_out, preferred_element_type=jnp.float32)
    normed_two, inverse_two = rms_forward(residual, gain_second)
    hidden_two = normed_two.astype(jnp.bfloat16)
    token_count = seq_count * block_len
    expert_count = weight_router.shape[1]
    flat_two = hidden_two.reshape(token_count, model_width)
    logits = jnp.dot(flat_two, weight_router, preferred_element_type=jnp.float32)
    router_prob = jax.nn.softmax(logits, axis=-1)
    chosen = expert_index.reshape(seq_count, block_len)
    choice_hot = (chosen[..., None] == jnp.arange(expert_count, dtype=jnp.int32)).astype(
        jnp.float32
    )
    flat_hot = choice_hot.reshape(token_count, expert_count)
    kept_rows = keep_mask.reshape(token_count).astype(jnp.float32)
    picked = jnp.sum(router_prob * flat_hot, axis=-1)
    gate_value = kept_rows * picked
    most_rows = max(2, (5 * block_len + 4 * expert_count - 1) // (4 * expert_count))
    capacity = seq_count * most_rows
    lower_tri = (jnp.arange(block_len)[:, None] >= jnp.arange(block_len)[None, :]).astype(
        jnp.float32
    )
    running = jnp.einsum("ij,sje->sie", lower_tri, choice_hot, precision=HIGHEST)
    slot_rank = (jnp.sum(running * choice_hot, axis=-1) - 1.0).astype(jnp.int32)
    token_slot = (
        chosen * capacity + jnp.arange(seq_count, dtype=jnp.int32)[:, None] * most_rows + slot_rank
    ).reshape(token_count)
    is_live = keep_mask.reshape(token_count) > 0
    target = jnp.where(is_live, token_slot, expert_count * capacity)
    safe_slot = jnp.where(is_live, token_slot, 0)
    shards = lax.axis_size("exp")
    local_count = expert_count // shards

    def dispatch(row_data):
        buffer = (
            jnp.zeros((expert_count * capacity, model_width), jnp.bfloat16)
            .at[target]
            .set(row_data, mode="drop")
        )
        return buffer.reshape(shards, local_count * capacity, model_width)

    def to_experts(arrived):
        return (
            arrived.reshape(shards, local_count, capacity, model_width)
            .transpose(1, 0, 2, 3)
            .reshape(local_count, shards * capacity, model_width)
        )

    def from_experts(row_data):
        return (
            row_data.reshape(local_count, shards, capacity, model_width)
            .transpose(1, 0, 2, 3)
            .reshape(shards, local_count * capacity, model_width)
        )

    arrived = lax.all_to_all(dispatch(flat_two), "exp", split_axis=0, concat_axis=0, tiled=True)
    expert_rows_in = to_experts(arrived)
    before = jnp.einsum(
        "lrd,ldf->lrf", expert_rows_in, weight_up, preferred_element_type=jnp.float32
    )
    activated, gelu_back = jax.vjp(jax.nn.gelu, before)
    acted_low = activated.astype(jnp.bfloat16)
    produced = jnp.einsum(
        "lrf,lfd->lrd", acted_low, weight_down, preferred_element_type=jnp.float32
    ).astype(jnp.bfloat16)
    returned = lax.all_to_all(
        from_experts(produced), "exp", split_axis=0, concat_axis=0, tiled=True
    )
    expert_rows = (
        returned.reshape(expert_count * capacity, model_width)[safe_slot].astype(jnp.float32)
        * kept_rows[:, None]
    )
    combined = residual.reshape(token_count, model_width) + gate_value[:, None] * expert_rows
    layer_out = combined.reshape(seq_count, block_len, model_width).astype(jnp.bfloat16)
    grad_top = cotangent.astype(jnp.float32).reshape(token_count, model_width)
    grad_result = (gate_value[:, None] * grad_top).astype(jnp.bfloat16)
    grad_arrived = lax.all_to_all(
        dispatch(grad_result), "exp", split_axis=0, concat_axis=0, tiled=True
    )
    grad_produced = to_experts(grad_arrived)
    grad_picked = jnp.sum(grad_top * expert_rows, axis=-1)
    grad_logits = (picked[:, None] * (flat_hot - router_prob) * grad_picked[:, None]).astype(
        jnp.bfloat16
    )
    grad_router = jnp.einsum("td,te->de", flat_two, grad_logits, preferred_element_type=jnp.float32)
    grad_hidden_two = jnp.einsum(
        "te,de->td", grad_logits, weight_router, preferred_element_type=jnp.float32
    )
    grad_acted = jnp.einsum(
        "lrd,lfd->lrf", grad_produced, weight_down, preferred_element_type=jnp.float32
    )
    grad_expert_down = jnp.einsum(
        "lrf,lrd->lfd", acted_low, grad_produced, preferred_element_type=jnp.float32
    )
    grad_before = gelu_back(grad_acted)[0].astype(jnp.bfloat16)
    grad_expert_up = jnp.einsum(
        "lrd,lrf->ldf", expert_rows_in, grad_before, preferred_element_type=jnp.float32
    )
    grad_inputs = jnp.einsum(
        "lrf,ldf->lrd", grad_before, weight_up, preferred_element_type=jnp.float32
    ).astype(jnp.bfloat16)
    grad_back = lax.all_to_all(
        from_experts(grad_inputs), "exp", split_axis=0, concat_axis=0, tiled=True
    )
    grad_hidden_two = (
        grad_hidden_two
        + grad_back.reshape(expert_count * capacity, model_width)[safe_slot].astype(jnp.float32)
        * kept_rows[:, None]
    )
    grad_residual, grad_gain_two = rms_backward(
        residual,
        inverse_two,
        gain_second,
        grad_hidden_two.reshape(seq_count, block_len, model_width),
    )
    grad_residual = grad_residual + grad_top.reshape(seq_count, block_len, model_width)
    grad_mixed = grad_residual.astype(jnp.bfloat16)
    grad_weight_out = jnp.einsum(
        "sbi,sbo->io", attended_low, grad_mixed, preferred_element_type=jnp.float32
    )
    grad_attended = jnp.einsum(
        "sbo,io->sbi", grad_mixed, weight_out, preferred_element_type=jnp.float32
    ).astype(jnp.bfloat16)
    grad_heads = grad_attended.reshape(seq_count, block_len, head_count, head_size)
    row_delta = jnp.einsum("sbhe,sbhe->shb", grad_heads.astype(jnp.float32), attended)
    grad_q, grad_off, grad_kv = attend_backward(
        queries, grad_heads, gathered, offset_values, logsum, row_delta, ctx_place
    )
    grad_kv = lax.psum_scatter(
        grad_kv.astype(jnp.bfloat16), "ctx", scatter_dimension=1, tiled=True
    ).astype(jnp.float32)
    grad_joint_low = jnp.concatenate(
        [grad_q.reshape(seq_count, block_len, model_width), grad_kv], axis=-1
    ).astype(jnp.bfloat16)
    grad_weight_joint = jnp.einsum(
        "sbi,sbo->io", hidden_one, grad_joint_low, preferred_element_type=jnp.float32
    )
    grad_hidden_one = jnp.einsum(
        "sbo,io->sbi", grad_joint_low, weight_joint, preferred_element_type=jnp.float32
    )
    grad_input_norm, grad_gain_one = rms_backward(
        tokens_f, inverse_one, gain_first, grad_hidden_one
    )
    grad_tokens = grad_input_norm + grad_residual
    grad_table = jnp.einsum("bo,ho->bh", bucket_hot, grad_off, precision=HIGHEST)
    dense_parts = (
        lax.psum_scatter(
            grad_gain_one.astype(jnp.bfloat16), "exp", scatter_dimension=0, tiled=True
        ).astype(jnp.float32),
        lax.psum_scatter(
            grad_weight_joint.astype(jnp.bfloat16), "exp", scatter_dimension=0, tiled=True
        ).astype(jnp.float32),
        lax.psum_scatter(
            grad_weight_out.astype(jnp.bfloat16), "exp", scatter_dimension=0, tiled=True
        ).astype(jnp.float32),
        lax.psum_scatter(
            grad_table.astype(jnp.bfloat16), "exp", scatter_dimension=0, tiled=True
        ).astype(jnp.float32),
        lax.psum_scatter(
            grad_gain_two.astype(jnp.bfloat16), "exp", scatter_dimension=0, tiled=True
        ).astype(jnp.float32),
        lax.psum_scatter(
            grad_router.astype(jnp.bfloat16), "exp", scatter_dimension=0, tiled=True
        ).astype(jnp.float32),
    )
    dense_parts = (
        lax.psum(dense_parts[0].astype(jnp.bfloat16), "ctx").astype(jnp.float32),
        lax.psum(dense_parts[1].astype(jnp.bfloat16), "ctx").astype(jnp.float32),
        lax.psum(dense_parts[2].astype(jnp.bfloat16), "ctx").astype(jnp.float32),
        lax.psum(dense_parts[3].astype(jnp.bfloat16), "ctx").astype(jnp.float32),
        lax.psum(dense_parts[4].astype(jnp.bfloat16), "ctx").astype(jnp.float32),
        lax.psum(dense_parts[5].astype(jnp.bfloat16), "ctx").astype(jnp.float32),
    )
    expert_parts = (
        lax.psum_scatter(
            grad_expert_up.astype(jnp.bfloat16), "ctx", scatter_dimension=2, tiled=True
        ).astype(jnp.float32),
        lax.psum_scatter(
            grad_expert_down.astype(jnp.bfloat16), "ctx", scatter_dimension=1, tiled=True
        ).astype(jnp.float32),
    )
    return (
        layer_out,
        grad_tokens,
        dense_parts[0],
        dense_parts[1],
        dense_parts[2],
        dense_parts[3],
        dense_parts[4],
        dense_parts[5],
        expert_parts[0],
        expert_parts[1],
    )


def solution(mesh):
    in_specs = (
        P("exp", "ctx", None),
        P("exp"),
        P("exp", None),
        P("exp", None),
        P("exp", None),
        P("exp"),
        P("exp", None),
        P("exp", None, "ctx"),
        P("exp", "ctx", None),
        P("exp", "ctx", None),
        P("exp", "ctx"),
        P(),
        P("exp", "ctx", None),
    )
    out_specs = (
        P("exp", "ctx", None),
        P("exp", "ctx", None),
        P("exp"),
        P("exp", None),
        P("exp", None),
        P("exp", None),
        P("exp"),
        P("exp", None),
        P("exp", None, "ctx"),
        P("exp", "ctx", None),
    )
    return jax.shard_map(
        per_device, mesh=mesh, in_specs=in_specs, out_specs=out_specs, check_vma=False
    )
```

profile of v0, /device:TPU:0, one launch (start us, length us, event | category | flops | bytes accessed | tf_op | source)
XLA Modules:
  0.0 1455.6 jit_solution(3617758443337259044)
XLA Ops:
  28.4 18.2 %all-gather.8.cloned.1.call-done = bf16[768,2304]{1,0:T(8,128)(2,1)} async-done(((bf16[96,2304]{1,0:T(8,128)(2,1)}), bf16[768,2304]{1,0:T(8,128)(2,1)}) %all-gather.8.cloned.1.call-update) | async-done | bytes 3538960 | tf_op jit(solution)/shard_map/all_gather | solution.py:188
  67.7 101.5 %all-gather.10.cloned.1.call-done = bf16[2,1024,1536]{2,1,0:T(8,128)(2,1)} async-done(((bf16[2,256,1536]{2,1,0:T(8,128)(2,1)}), bf16[2,1024,1536]{2,1,0:T(8,128)(2,1)}) %all-gather.10.cloned.1.call-update) | async-done | bytes 6291472 | tf_op jit(solution)/shard_map/all_gather | solution.py:212
  177.9 150.3 %while.60 = (s32[]{:T(128)}, f32[2,12,256]{2,1,0:T(8,128)S(1)}, f32[2,12,256]{2,1,0:T(8,128)S(1)}, bf16[2,1024,1536]{1,2,0:T(8,128)(2,1)}, bf16[2,256,12,64]{1,3...) while((s32[]{:T(128)}, f32[2,12,256]{2,1,0:T(8,128)S(1)}, ...), condition=%wide.region_4.0_spmd.clone, body=%wide.region_1.0_spmd.clone.sunk | while | flops 424704000 | bytes 159940752 | solution.py:101
  184.0 16.6 %reshape.597 = f32[12,196352]{1,0:T(8,128)} reshape(f32[12,256,767]{2,1,0:T(8,128)} %broadcast_in_dim.143) | data formatting | bytes 18849792 | tf_op jit(solution)/shard_map/while/body/eval_jaxpr/reshape | solution.py:30
  212.8 20.5 %reshape.598 = f32[12,256,766]{2,1,0:T(8,128)} reshape(f32[12,196096]{1,0:T(8,128)} %slice.180) | data formatting | bytes 18825216 | tf_op jit(solution)/shard_map/while/body/eval_jaxpr/reshape | solution.py:33
  259.4 16.6 %reshape.597 = f32[12,196352]{1,0:T(8,128)} reshape(f32[12,256,767]{2,1,0:T(8,128)} %broadcast_in_dim.143) | data formatting | bytes 18849792 | tf_op jit(solution)/shard_map/while/body/eval_jaxpr/reshape | solution.py:30
  287.7 20.5 %reshape.598 = f32[12,256,766]{2,1,0:T(8,128)} reshape(f32[12,196096]{1,0:T(8,128)} %slice.180) | data formatting | bytes 18825216 | tf_op jit(solution)/shard_map/while/body/eval_jaxpr/reshape | solution.py:33
  328.2 169.1 %while.61 = (s32[]{:T(128)}, f32[2,256,12,64]{1,3,2,0:T(8,128)}, bf16[2,1024,1536]{1,2,0:T(8,128)(2,1)}, bf16[2,256,12,64]{1,3,2,0:T(8,128)(2,1)S(1)}, s32[]{:T(...) while((s32[]{:T(128)}, f32[2,256,12,64]{1,3,2,0:T(8,128)}, ...), condition=%wide.region_6.0_spmd.clone, body=%wide.region_5.0_spmd.clone.sunk | while | flops 818675712 | bytes 110887040 | solution.py:113
  349.3 16.6 %reshape.599 = f32[12,196352]{1,0:T(8,128)} reshape(f32[12,256,767]{2,1,0:T(8,128)} %broadcast_in_dim.144) | data formatting | bytes 18849792 | tf_op jit(solution)/shard_map/while/body/eval_jaxpr/reshape | solution.py:30
  377.6 20.5 %reshape.600 = f32[12,256,766]{2,1,0:T(8,128)} reshape(f32[12,196096]{1,0:T(8,128)} %slice.182) | data formatting | bytes 18825216 | tf_op jit(solution)/shard_map/while/body/eval_jaxpr/reshape | solution.py:33
  455.1 20.5 %reshape.600 = f32[12,256,766]{2,1,0:T(8,128)} reshape(f32[12,196096]{1,0:T(8,128)} %slice.182) | data formatting | bytes 18825216 | tf_op jit(solution)/shard_map/while/body/eval_jaxpr/reshape | solution.py:33
  510.9 17.2 %all-gather.1 = bf16[8,96,8]{1,2,0:T(8,128)(2,1)S(1)} all-gather(bf16[1,96,8]{1,2,0:T(8,128)(2,1)S(1)} %bitcast.282), channel_id=1, replica_groups=mesh['ctx'=4,'exp'=8] {'exp'}, dimensions={0}, use_global_device_ids=true | all-gather | bytes 13824 | tf_op jit(solution)/shard_map/all_gather | solution.py:192
  614.7 375.1 %while.62 = (s32[]{:T(128)}, f32[2,256,12,64]{1,3,2,0:T(8,128)}, f32[12,2047]{1,0:T(8,128)S(1)}, bf16[2,1024,1536]{2,1,0:T(8,128)(2,1)}, bf16[2,1024,1536]{1,2,0...) while((s32[]{:T(128)}, f32[2,256,12,64]{1,3,2,0:T(8,128)}, ...), condition=%wide.region_19.20_spmd.clone, body=%wide.region_16.19_spmd.clone.sunk | while | flops 2060448768 | bytes 347725920 | solution.py:165
  652.7 20.9 %reshape.602 = f32[12,256,766]{2,1,0:T(8,128)} reshape(f32[12,196096]{1,0:T(8,128)} %slice.184) | data formatting | bytes 18825216 | tf_op jit(solution)/shard_map/while/body/eval_jaxpr/reshape | solution.py:33
  772.5 20.2 %reshape.604 = f32[12,256,767]{2,1,0:T(8,128)} reshape(f32[12,196352]{1,0:T(8,128)} %pad.54) | data formatting | bytes 18849792 | tf_op jit(solution)/shard_map/while/body/eval_jaxpr/reshape | solution.py:46
  835.8 20.6 %reshape.602 = f32[12,256,766]{2,1,0:T(8,128)} reshape(f32[12,196096]{1,0:T(8,128)} %slice.184) | data formatting | bytes 18825216 | tf_op jit(solution)/shard_map/while/body/eval_jaxpr/reshape | solution.py:33
  957.0 20.4 %reshape.604 = f32[12,256,767]{2,1,0:T(8,128)} reshape(f32[12,196352]{1,0:T(8,128)} %pad.54) | data formatting | bytes 18849792 | tf_op jit(solution)/shard_map/while/body/eval_jaxpr/reshape | solution.py:46
  1019.4 77.8 %reduce-scatter.9.cloned.1.call-done = bf16[2,256,1536]{2,1,0:T(8,128)(2,1)} async-done(((bf16[2,1024,1536]{2,1,0:T(8,128)(2,1)}), bf16[2,256,1536]{2,1,0:T(8,128)(2,1)}) %reduce-scatter.9.cloned.1.call-update) | async-done | bytes 1572880 | tf_op jit(solution)/shard_map/reduce_scatter | solution.py:346
  1104.7 30.2 %reduce-scatter.19.cloned.1.call-done = bf16[96,8]{1,0:T(8,128)(2,1)} async-done(((bf16[768,8]{1,0:T(8,128)(2,1)}), bf16[96,8]{1,0:T(8,128)(2,1)}) %reduce-scatter.19.cloned.1.call-update) | async-done | bytes 1552
  1135.7 86.9 %reduce-scatter.17.cloned.1.call-done = bf16[1,768,768]{2,1,0:T(8,128)(2,1)} async-done(((bf16[1,3072,768]{2,1,0:T(8,128)(2,1)}), bf16[1,768,768]{2,1,0:T(8,128)(2,1)}) %reduce-scatter.17.cloned.1.call-update) | async-done | bytes 1179664 | tf_op jit(solution)/shard_map/reduce_scatter | solution.py:395
  1225.4 85.4 %reduce-scatter.15.cloned.1.call-done = bf16[1,768,768]{2,1,0:T(8,128)(2,1)} async-done(((bf16[1,768,3072]{2,1,0:T(8,128)(2,1)}), bf16[1,768,768]{2,1,0:T(8,128)(2,1)}) %reduce-scatter.15.cloned.1.call-update) | async-done | bytes 1179664 | tf_op jit(solution)/shard_map/reduce_scatter | solution.py:392
  1319.4 24.2 %all-reduce.7 = (bf16[768]{0:T(1024)(128)(2,1)S(1)}, bf16[32,12]{1,0:T(8,128)(2,1)S(1)}, bf16[768]{0:T(1024)(128)(2,1)S(1)}) all-reduce(bf16[768]{0:T(1024)(128)(2,1)S(1)} %get-tuple-element.1010, bf16[32,12]{1,0:T(8,128)(2,1)S(1)} %convolution_convert_fusion.5, ...), channel_id=3, replica_groups=mesh['ctx'=4,'exp'=8] {'exp'}, use_global_device_ids=true, to_apply=%region_23.24.clone | all-reduce | flops 1920 | bytes 7680
  1351.6 51.6 %reduce-scatter.11.cloned.1.call-done = bf16[96,2304]{1,0:T(8,128)(2,1)} async-done(((bf16[768,2304]{1,0:T(8,128)(2,1)}), bf16[96,2304]{1,0:T(8,128)(2,1)}) %reduce-scatter.11.cloned.1.call-update) | async-done | bytes 442384 | tf_op jit(solution)/shard_map/reduce_scatter | solution.py:367
  1420.3 24.6 %all-reduce.13.cloned.1.call-done = (bf16[96,2304]{1,0:T(8,128)(2,1)}, bf16[96,768]{1,0:T(8,128)(2,1)}) async-done(((bf16[96,2304]{1,0:T(8,128)(2,1)}, bf16[96,768]{1,0:T(8,128)(2,1)}), (bf16[96,2304]{1,0:T(8,128)(2,1)}, bf16[96,768]{1,0:T(8,128)(2,1)})) %all-reduce.13.cloned.1.call-update) | async-done | bytes 589840 | tf_op jit(solution)/shard_map/psum | solution.py:385
  (360 shorter events, 684.5 us)
Async XLA Ops:
  7.2 39.5 %all-gather.8.cloned.1.call-start = ((), (), s32[]{:S(2)}) async-start(), calls=%async_computation.10 | async-start | bytes 3981312 | tf_op jit(solution)/shard_map/all_gather | solution.py:188
  7.9 161.3 %all-gather.10.cloned.1.call-start = ((), (), s32[]{:S(2)}) async-start(), calls=%async_computation.11 | async-start | bytes 7864320 | tf_op jit(solution)/shard_map/all_gather | solution.py:212
  53.7 445.3 %all-gather.12.cloned.1.call-start = ((), (), s32[]{:S(2)}) async-start(), calls=%async_computation.12 | async-start | bytes 1327104 | tf_op jit(solution)/shard_map/all_gather | solution.py:189
  54.4 484.1 %all-gather.14.cloned.1.call-start = ((), (), s32[]{:S(2)}) async-start(), calls=%async_computation.13 | async-start | bytes 5898240 | tf_op jit(solution)/shard_map/all_gather | solution.py:195
  55.0 491.1 %all-gather.16.cloned.1.call-start = ((), (), s32[]{:S(2)}) async-start(), calls=%async_computation.14 | async-start | bytes 5898240 | tf_op jit(solution)/shard_map/all_gather | solution.py:196
  328.2 170.8 %copy-start.22 = (bf16[2,256,768]{2,1,0:T(8,128)(2,1)S(1)}, bf16[2,256,768]{2,1,0:T(8,128)(2,1)}, u32[]{:S(2)}) copy-start(bf16[2,256,768]{2,1,0:T(8,128)(2,1)} %param.19) | copy-start | bytes 2359300
  506.7 27.4 %all-to-all-start = ((bf16[8,80,768]{2,1,0:T(8,128)(2,1)}), bf16[8,80,768]{2,1,0:T(8,128)(2,1)S(1)}, u32[]{:S(2)}, u32[]{:S(2)}) async-start(bf16[8,80,768]{2,1,0:T(8,128)(2,1)} %bitcast.17), calls=%async_computation | async-start | bytes 1966080 | tf_op jit(solution)/shard_map/all_to_all | solution.py:273
  528.6 72.6 %copy-start.27 = (f32[512,8]{0,1:T(8,128)}, f32[512,8]{0,1:T(8,128)S(1)}, u32[]{:S(2)}) copy-start(f32[512,8]{0,1:T(8,128)S(1)} %get-tuple-element.1094) | copy-start | bytes 49156
  534.0 22.3 %all-to-all-start.2 = ((bf16[8,80,768]{2,1,0:T(8,128)(2,1)}), bf16[8,80,768]{2,1,0:T(8,128)(2,1)}, u32[]{:S(2)}, u32[]{:S(2)}) async-start(bf16[8,80,768]{2,1,0:T(8,128)(2,1)} %bitcast.26), calls=%async_computation.2 | async-start | bytes 1966080 | tf_op jit(solution)/shard_map/all_to_all | solution.py:294
  556.3 23.0 %all-to-all-start.1 = ((bf16[8,80,768]{2,1,0:T(8,128)(2,1)}), bf16[8,80,768]{2,1,0:T(8,128)(2,1)S(1)}, u32[]{:S(2)}, u32[]{:S(2)}) async-start(bf16[8,80,768]{2,1,0:T(8,128)(2,1)} %bitcast.21), calls=%async_computation.1 | async-start | bytes 1966080 | tf_op jit(solution)/shard_map/all_to_all | solution.py:283
  579.3 18.9 %all-to-all-start.3 = ((bf16[8,80,768]{2,1,0:T(8,128)(2,1)}), bf16[8,80,768]{2,1,0:T(8,128)(2,1)S(1)}, u32[]{:S(2)}, u32[]{:S(2)}) async-start(bf16[8,80,768]{2,1,0:T(8,128)(2,1)} %bitcast.267), calls=%async_computation.3 | async-start | bytes 1966080 | tf_op jit(solution)/shard_map/all_to_all | solution.py:319
  583.5 513.7 %reduce-scatter.9.cloned.1.call-start = ((), (), s32[]{:S(2)}) async-start(), calls=%async_computation.15 | async-start | bytes 7864320 | tf_op jit(solution)/shard_map/reduce_scatter | solution.py:346
  615.0 71.3 %copy-start.2 = (bf16[2,256,12,64]{1,3,2,0:T(8,128)(2,1)}, bf16[2,256,12,64]{1,3,2,0:T(8,128)(2,1)S(1)}, u32[]{:S(2)}) copy-start(bf16[2,256,12,64]{1,3,2,0:T(8,128)(2,1)S(1)} %get-tuple-element.1389) | copy-start | bytes 2359300 | tf_op jit(solution)/shard_map/while
  798.1 71.1 %copy-start.2 = (bf16[2,256,12,64]{1,3,2,0:T(8,128)(2,1)}, bf16[2,256,12,64]{1,3,2,0:T(8,128)(2,1)S(1)}, u32[]{:S(2)}) copy-start(bf16[2,256,12,64]{1,3,2,0:T(8,128)(2,1)S(1)} %get-tuple-element.1389) | copy-start | bytes 2359300 | tf_op jit(solution)/shard_map/while
  989.9 144.9 %reduce-scatter.19.cloned.1.call-start = ((), (), s32[]{:S(2)}) async-start(), calls=%async_computation.20 | async-start | bytes 221184
  992.1 230.5 %reduce-scatter.17.cloned.1.call-start = ((), (), s32[]{:S(2)}) async-start(), calls=%async_computation.19 | async-start | bytes 5898240 | tf_op jit(solution)/shard_map/reduce_scatter | solution.py:395
  1003.5 307.2 %reduce-scatter.15.cloned.1.call-start = ((), (), s32[]{:S(2)}) async-start(), calls=%async_computation.18 | async-start | bytes 5898240 | tf_op jit(solution)/shard_map/reduce_scatter | solution.py:392
  1012.4 84.8 %copy-start.58 = (f32[768]{0:T(1024)S(1)}, f32[768]{0:T(1024)}, u32[]{:S(2)}) copy-start(f32[768]{0:T(1024)} %copy-done.57) | copy-start | bytes 9220
  1012.4 84.8 %copy-start.60 = (f32[2,256]{1,0:T(2,128)S(1)}, f32[2,256]{1,0:T(2,128)}, u32[]{:S(2)}) copy-start(f32[2,256]{1,0:T(2,128)} %copy-done.59) | copy-start | bytes 6148
  1012.4 339.2 %reduce-scatter.13.cloned.1.call-start = ((), (), s32[]{:S(2)}) async-start(), calls=%async_computation.17 | async-start | bytes 1327104 | tf_op jit(solution)/shard_map/reduce_scatter | solution.py:370
  1016.8 386.4 %reduce-scatter.11.cloned.1.call-start = ((), (), s32[]{:S(2)}) async-start(), calls=%async_computation.16 | async-start | bytes 3981312 | tf_op jit(solution)/shard_map/reduce_scatter | solution.py:367
  1019.4 85.1 %copy-start.47 = (s32[2047]{0:T(1024)S(1)}, s32[2047]{0:T(1024)}, u32[]{:S(2)}) copy-start(s32[2047]{0:T(1024)} %param.30) | copy-start | bytes 24568
  1102.8 210.9 %copy-start.23 = (bf16[2,256,768]{2,1,0:T(8,128)(2,1)S(1)}, bf16[2,256,768]{2,1,0:T(8,128)(2,1)}, u32[]{:S(2)}) copy-start(bf16[2,256,768]{2,1,0:T(8,128)(2,1)} %param.19) | copy-start | bytes 2359300
  1102.8 342.1 %all-reduce.13.cloned.1.call-start = ((), (), s32[]{:S(2)}) async-start(), calls=%async_computation.21 | async-start | bytes 1179648 | tf_op jit(solution)/shard_map/psum | solution.py:385
  (67 other events, 508.4 us)
Sparse Core Ops, SparseCore 0:
  9.9 36.6 all-gather.7
  53.8 115.3 all-gather.9
  171.1 22.2 all-gather.11
  194.8 89.3 all-gather.13
  285.7 87.8 all-gather.15
  990.0 107.1 reduce-scatter.8
  1100.8 34.0 reduce-scatter.18
  1137.3 85.2 reduce-scatter.16
  1225.0 85.7 reduce-scatter.14
  1314.2 37.3 reduce-scatter.12
  1355.1 48.0 reduce-scatter.10
  1405.5 39.3 all-reduce.12
where the time goes:
time: 1460 us
  local copies, waits for them, and re-layouts  599 us (41%)
  waiting for transfers between devices  493 us (34%)
  matrix products  181 us (12%)
  blocking collectives  77.2 us (5%)
  other arithmetic  48 us (3%)
  loops' own time  22.5 us (2%)
  between operations  17.4 us (1%)
  starting transfers between devices  17.2 us (1%)
    reshape x6, local copies, waits for them, and re-layouts, bias_block(): tiled[:, row_count - 1:row_count - 1 + row_count * (span - 1)]  123 us
    all_gather x1, waiting for transfers between devices, per_device(): gathered = lax.all_gather(key_values, 'ctx', axis=1, tiled=True)  101 us
    reshape x6, local copies, waits for them, and re-layouts, bias_block(): jnp.broadcast_to(window[:, None, :], (head_count, row_count, span))  99.7 us
    reduce_scatter x1, waiting for transfers between devices, per_device(): lax.psum_scatter(grad_expert_down.astype(jnp.bfloat16), 'ctx', scatter_di...  86.9 us
    reduce_scatter x1, waiting for transfers between devices, per_device(): lax.psum_scatter(grad_expert_up.astype(jnp.bfloat16), 'ctx', scatter_dime...  85.4 us
    reduce_scatter x1, waiting for transfers between devices, per_device(): lax.psum_scatter(grad_kv.astype(jnp.bfloat16), 'ctx', scatter_dimension=1...  77.8 us
    slice x12, local copies, waits for them, and re-layouts, bias_block(): return skewed[:, :, :col_count]  76.2 us
    slice x6, local copies, waits for them, and re-layouts, bias_block(): tiled[:, row_count - 1:row_count - 1 + row_count * (span - 1)]  70.5 us
  transfers between devices with their start and end apart: 16, of which 10 were waited for; matrix products, arithmetic and copies ran while one was open for 29% of the time, Pallas kernels for 0%

commit v1 on v0

v1 whole, which is shorter than its diff:
```python
import functools

import jax
import jax.numpy as jnp
from jax import lax
from jax.experimental import pallas as pl
from jax.experimental.pallas import tpu as pltpu
from jax.sharding import PartitionSpec as P

EPSILON = 1e-06
HALF = 64
TILE = 128
GROUP = 256
VMEM_BYTES = 50 * 1024 * 1024
SCORE_SCALE = 0.125
HIGHEST = lax.Precision.HIGHEST
BOTH = ("ctx", "exp")


def contract_last(left, right):
    return lax.dot_general(
        left, right, (((1,), (1,)), ((), ())), preferred_element_type=jnp.float32
    )


def matmul(left, right):
    return lax.dot_general(
        left, right, (((1,), (0,)), ((), ())), preferred_element_type=jnp.float32
    )


def skew_kernel(offset_ref, skew_ref):
    padded = offset_ref.shape[-1]
    kept = skew_ref.shape[1]
    rows = jnp.broadcast_to(offset_ref[0], (TILE, padded))
    rolled = pltpu.roll(rows, padded - (TILE - 1), 1, stride=1, stride_axis=0)
    skew_ref[0] = rolled[:, :kept].T.astype(skew_ref.dtype)


def make_skew(offset_values):
    head_count, padded = offset_values.shape
    kept = padded - TILE
    return pl.pallas_call(
        skew_kernel,
        grid=(head_count,),
        in_specs=[pl.BlockSpec((1, 1, padded), lambda h: (h, 0, 0))],
        out_specs=pl.BlockSpec((1, kept, TILE), lambda h: (h, 0, 0)),
        out_shape=jax.ShapeDtypeStruct((head_count, kept, TILE), jnp.bfloat16),
        compiler_params=pltpu.CompilerParams(vmem_limit_bytes=VMEM_BYTES),
        name="skew_bias",
    )(offset_values.reshape(head_count, 1, padded))


def half_mask(rows, half):
    lanes = lax.broadcasted_iota(jnp.int32, (rows, TILE), 1)
    return (lanes // HALF) == half


def bias_rows(key_base, query_base, seq_len):
    return key_base - query_base + seq_len - TILE


def forward_kernel(
    base_ref, q_ref, k_ref, v_ref, skew_ref, out_ref, lse_ref, score_ref, prob_ref, *, chunk
):
    query_rows = q_ref.shape[0]
    key_rows = k_ref.shape[0]
    seq_len = key_rows
    mask = [half_mask(GROUP, 0), half_mask(GROUP, 1)]
    value_t = v_ref[...].T
    for group in range(query_rows // GROUP):
        rows = slice(group * GROUP, (group + 1) * GROUP)
        query_base = base_ref[0] + group * GROUP
        halves = []
        for half in range(2):
            queries = jnp.where(mask[half], q_ref[rows], 0).astype(jnp.bfloat16)
            score_ref[half] = contract_last(k_ref[...], queries)
            top = jnp.full((8, GROUP), -jnp.inf, jnp.float32)
            for start in range(0, key_rows, chunk):
                key_base = base_ref[start // query_rows] + start % query_rows
                place = pl.multiple_of(bias_rows(key_base, query_base, seq_len), TILE)
                left = skew_ref[half, pl.ds(place, chunk), :]
                right = skew_ref[half, pl.ds(place - TILE, chunk), :]
                bias = jnp.concatenate([left, right], axis=1).astype(jnp.float32)
                piece = score_ref[half, start : start + chunk] + bias
                score_ref[half, start : start + chunk] = piece
                top = jnp.maximum(top, jnp.max(piece.reshape(chunk // 8, 8, GROUP), axis=0))
            top = jnp.max(top, axis=0, keepdims=True)
            total = jnp.zeros((8, GROUP), jnp.float32)
            for start in range(0, key_rows, chunk):
                piece = jnp.exp(score_ref[half, start : start + chunk] - top)
                total = total + jnp.sum(piece.reshape(chunk // 8, 8, GROUP), axis=0)
                prob_ref[half, start : start + chunk] = piece.astype(jnp.bfloat16)
            total = jnp.sum(total, axis=0, keepdims=True)
            lse_ref[0, half : half + 1, rows] = top + jnp.log(total)
            mixed = matmul(value_t[half * HALF : (half + 1) * HALF], prob_ref[half])
            halves.append(mixed / total)
        out_ref[rows] = jnp.concatenate(halves, axis=0).T


def attend_forward(bases, queries, key_values, skew):
    query_rows, width = queries.shape
    key_rows = key_values.shape[0]
    kept = skew.shape[1]
    pairs = width // TILE
    chunk = TILE
    return pl.pallas_call(
        functools.partial(forward_kernel, chunk=chunk),
        grid_spec=pltpu.PrefetchScalarGridSpec(
            num_scalar_prefetch=1,
            grid=(pairs,),
            in_specs=[
                pl.BlockSpec((query_rows, TILE), lambda p, _: (0, p)),
                pl.BlockSpec((key_rows, TILE), lambda p, _: (0, p)),
                pl.BlockSpec((key_rows, TILE), lambda p, _: (0, p + pairs)),
                pl.BlockSpec((2, kept, TILE), lambda p, _: (p, 0, 0)),
            ],
            out_specs=[
                pl.BlockSpec((query_rows, TILE), lambda p, _: (0, p)),
                pl.BlockSpec((1, 2, query_rows), lambda p, _: (p, 0, 0)),
            ],
            scratch_shapes=[
                pltpu.VMEM((2, key_rows, GROUP), jnp.float32),
                pltpu.VMEM((2, key_rows, GROUP), jnp.bfloat16),
            ],
        ),
        out_shape=[
            jax.ShapeDtypeStruct((query_rows, width), jnp.float32),
            jax.ShapeDtypeStruct((pairs, 2, query_rows), jnp.float32),
        ],
        compiler_params=pltpu.CompilerParams(vmem_limit_bytes=VMEM_BYTES),
        name="attend_forward",
    )(bases, queries, key_values, key_values, skew)


def backward_kernel(
    base_ref, q_ref, do_ref, o_ref, k_ref, v_ref, skew_ref, lse_ref,
    dq_ref, dk_ref, dv_ref, off_ref,
    score_ref, gradp_ref, prob_ref, grads_ref, accum_k, accum_v, accum_skew,
    *, chunk,
):
    query_rows = q_ref.shape[0]
    key_rows = k_ref.shape[0]
    seq_len = key_rows
    mask = [half_mask(GROUP, 0), half_mask(GROUP, 1)]
    key_t = k_ref[...].T
    accum_skew[...] = jnp.zeros_like(accum_skew)
    for group in range(query_rows // GROUP):
        rows = slice(group * GROUP, (group + 1) * GROUP)
        query_base = base_ref[0] + group * GROUP
        product = (do_ref[rows].astype(jnp.float32) * o_ref[rows]).T
        halves = []
        sum_k = None
        for half in range(2):
            queries = jnp.where(mask[half], q_ref[rows], 0).astype(jnp.bfloat16)
            grads_out = jnp.where(mask[half], do_ref[rows], 0).astype(jnp.bfloat16)
            score_ref[half] = contract_last(k_ref[...], queries)
            gradp_ref[half] = contract_last(v_ref[...], grads_out)
            logsum = lse_ref[0, half : half + 1, rows]
            delta = jnp.sum(product[half * HALF : (half + 1) * HALF], axis=0, keepdims=True)
            for start in range(0, key_rows, chunk):
                key_base = base_ref[start // query_rows] + start % query_rows
                place = pl.multiple_of(bias_rows(key_base, query_base, seq_len), TILE)
                here = pl.ds(start, chunk)
                left = skew_ref[half, pl.ds(place, chunk), :]
                right = skew_ref[half, pl.ds(place - TILE, chunk), :]
                bias = jnp.concatenate([left, right], axis=1).astype(jnp.float32)
                prob = jnp.exp(score_ref[half, here] + bias - logsum)
                grads = prob * (gradp_ref[half, here] - delta)
                prob_ref[half, here] = prob.astype(jnp.bfloat16)
                grads_ref[half, here] = grads.astype(jnp.bfloat16)
                accum_skew[half, pl.ds(place, chunk), :] += grads[:, :TILE]
                accum_skew[half, pl.ds(place - TILE, chunk), :] += grads[:, TILE:]
            part_k = matmul(grads_ref[half], queries)
            part_v = matmul(prob_ref[half], grads_out)
            sum_k = part_k if sum_k is None else sum_k + part_k
            sum_v = part_v if half == 0 else sum_v + part_v
            halves.append(matmul(key_t[half * HALF : (half + 1) * HALF], grads_ref[half]))
        if group == 0:
            accum_k[...] = sum_k
            accum_v[...] = sum_v
        else:
            accum_k[...] += sum_k
            accum_v[...] += sum_v
        dq_ref[rows] = (jnp.concatenate(halves, axis=0) * 0.125).T.astype(dq_ref.dtype)
    dk_ref[...] = accum_k[...].astype(dk_ref.dtype)
    dv_ref[...] = accum_v[...].astype(dv_ref.dtype)
    for half in range(2):
        turned = accum_skew[half].T
        padded = turned.shape[1]
        count = TILE // 2
        while count:
            turned = turned[:count] + pltpu.roll(turned[count : 2 * count], padded - count, 1)
            count //= 2
        off_ref[0, half : half + 1] = pltpu.roll(turned, TILE - 1, 1)


def attend_backward(bases, queries, grads_out, outputs, key_values, skew, logsum):
    query_rows, width = queries.shape
    key_rows = key_values.shape[0]
    kept = skew.shape[1]
    pairs = width // TILE
    chunk = TILE
    column = lambda count: pl.BlockSpec((count, TILE), lambda p, _: (0, p))
    return pl.pallas_call(
        functools.partial(backward_kernel, chunk=chunk),
        grid_spec=pltpu.PrefetchScalarGridSpec(
            num_scalar_prefetch=1,
            grid=(pairs,),
            in_specs=[
                column(query_rows), column(query_rows), column(query_rows),
                column(key_rows),
                pl.BlockSpec((key_rows, TILE), lambda p, _: (0, p + pairs)),
                pl.BlockSpec((2, kept, TILE), lambda p, _: (p, 0, 0)),
                pl.BlockSpec((1, 2, query_rows), lambda p, _: (p, 0, 0)),
            ],
            out_specs=[
                column(query_rows), column(key_rows), column(key_rows),
                pl.BlockSpec((1, 2, kept + TILE), lambda p, _: (p, 0, 0)),
            ],
            scratch_shapes=[
                pltpu.VMEM((2, key_rows, GROUP), jnp.float32),
                pltpu.VMEM((2, key_rows, GROUP), jnp.float32),
                pltpu.VMEM((2, key_rows, GROUP), jnp.bfloat16),
                pltpu.VMEM((2, key_rows, GROUP), jnp.bfloat16),
                pltpu.VMEM((key_rows, TILE), jnp.float32),
                pltpu.VMEM((key_rows, TILE), jnp.float32),
                pltpu.VMEM((2, kept + TILE, TILE), jnp.float32),
            ],
        ),
        out_shape=[
            jax.ShapeDtypeStruct((query_rows, width), jnp.bfloat16),
            jax.ShapeDtypeStruct((key_rows, width), jnp.bfloat16),
            jax.ShapeDtypeStruct((key_rows, width), jnp.bfloat16),
            jax.ShapeDtypeStruct((pairs, 2, kept + TILE), jnp.float32),
        ],
        compiler_params=pltpu.CompilerParams(vmem_limit_bytes=VMEM_BYTES),
        name="attend_backward",
    )(bases, queries, grads_out, outputs, key_values, key_values, skew, logsum)


def rms_forward(row_data, gain_vec):
    inverse = lax.rsqrt(jnp.mean(row_data * row_data, axis=-1, keepdims=True) + EPSILON)
    return (row_data * inverse * gain_vec, inverse)


def rms_backward(row_data, inverse, gain_vec, grad_out):
    normed = row_data * inverse
    grad_gain = jnp.sum(grad_out * normed, axis=0)
    scaled = grad_out * gain_vec
    spread = jnp.mean(scaled * normed, axis=-1, keepdims=True)
    return (inverse * (scaled - normed * spread), grad_gain)


class Layout:
    def __init__(self):
        self.ctx_count = lax.axis_size("ctx")
        self.exp_count = lax.axis_size("exp")
        self.span = self.ctx_count // 4
        self.members = 2 * self.span
        self.ctx = lax.axis_index("ctx")
        self.core = lax.axis_index("exp") % 2
        self.member = (self.ctx % self.span) * 2 + self.core
        self.side = (self.ctx // self.span) % 2

    def number(self, ctx, exp):
        return ctx * self.exp_count + exp

    def round_pairs(self, turn):
        pairs = []
        for ctx in range(self.ctx_count):
            for exp in range(self.exp_count):
                seq = 2 * (exp % 2) + (turn + ctx) % 2
                member = ctx // 2
                target = self.number(seq * self.span + member // 2, exp // 2 * 2 + member % 2)
                pairs.append((self.number(ctx, exp), target))
        return pairs

    def member_pairs(self, shift):
        pairs = []
        for ctx in range(self.ctx_count):
            for exp in range(self.exp_count):
                start = ctx // self.span * self.span
                member = ((ctx - start) * 2 + exp % 2 + shift) % self.members
                target = self.number(start + member // 2, exp // 2 * 2 + member % 2)
                pairs.append((self.number(ctx, exp), target))
        return pairs

    def gather_blocks(self, blocks):
        got = [
            lax.ppermute(
                lax.dynamic_index_in_dim(blocks, (turn + self.ctx) % 2, 0, keepdims=False),
                BOTH,
                self.round_pairs(turn),
            )
            for turn in range(2)
        ]
        first = jnp.where(self.side == 0, got[0], got[1])
        second = jnp.where(self.side == 0, got[1], got[0])
        return jnp.concatenate([first, second], axis=0)

    def return_blocks(self, rows):
        blocks = rows.reshape((2, rows.shape[0] // 2) + rows.shape[1:])
        got = [
            lax.ppermute(
                lax.dynamic_index_in_dim(blocks, (turn + self.side) % 2, 0, keepdims=False),
                BOTH,
                [(target, source) for source, target in self.round_pairs(turn)],
            )
            for turn in range(2)
        ]
        even = self.ctx % 2 == 0
        return jnp.stack([jnp.where(even, got[0], got[1]), jnp.where(even, got[1], got[0])])

    def all_rows(self, rows):
        return jnp.concatenate(
            [rows]
            + [lax.ppermute(rows, BOTH, self.member_pairs(shift)) for shift in range(1, self.members)],
            axis=0,
        )

    def sum_rows(self, partial):
        parts = partial.reshape((self.members, partial.shape[0] // self.members) + partial.shape[1:])
        total = parts[0]
        for shift in range(1, self.members):
            moved = lax.ppermute(
                parts[shift].astype(jnp.bfloat16), BOTH, self.member_pairs(self.members - shift)
            )
            total = total + moved.astype(jnp.float32)
        return total

    def bases(self, row_count):
        return jnp.stack(
            [(self.member - shift) % self.members * row_count for shift in range(self.members)]
        ).astype(jnp.int32)

    def swap(self, rows, distance):
        pairs = [(ctx, ctx ^ distance) for ctx in range(self.ctx_count)]
        return lax.ppermute(rows, "ctx", pairs)


def per_device(
    tokens_in,
    first_gain,
    joint_projection,
    out_projection,
    bias_table,
    second_gain,
    router_weight,
    expert_up,
    expert_down,
    expert_index,
    keep_mask,
    buckets,
    cotangent,
):
    layout = Layout()
    shards = layout.exp_count
    seq_count, block_len, model_width = tokens_in.shape
    token_count = seq_count * block_len
    expert_count = router_weight.shape[1]
    bucket_count = bias_table.shape[0] * shards
    head_count = bias_table.shape[1]

    small = [first_gain, second_gain, router_weight, bias_table]
    small_sizes = [part.size for part in small]
    small_full = lax.all_gather(
        jnp.concatenate([part.reshape(-1) for part in small]), "exp", axis=0, tiled=False
    )
    small_cuts = [sum(small_sizes[:place]) for place in range(1, len(small))]
    gain_one, gain_two, weight_router, table = jnp.split(small_full, small_cuts, axis=1)
    weight_router = weight_router.reshape(model_width, expert_count)
    table = table.reshape(bucket_count, head_count)
    gain_first = gain_one.reshape(model_width).astype(jnp.float32)
    gain_second = gain_two.reshape(model_width).astype(jnp.float32)
    weight_joint = lax.all_gather(joint_projection, "exp", axis=0, tiled=True)
    weight_out = lax.all_gather(out_projection, "exp", axis=0, tiled=True)

    tokens = layout.gather_blocks(tokens_in)
    every_token = layout.all_rows(tokens)
    codes = layout.gather_blocks(expert_index.reshape(seq_count, block_len) * 2 + keep_mask)
    grad_out_low = layout.gather_blocks(cotangent)
    chosen = codes // 2
    kept = codes % 2

    held_up, held_down, _ = lax.optimization_barrier((expert_up[0], expert_down[0], every_token))
    distances = range(0, layout.ctx_count, 2)
    ups = [held_up if step == 0 else layout.swap(held_up, step) for step in distances]
    downs = [held_down if step == 0 else layout.swap(held_down, step) for step in distances]

    offset_count = buckets.shape[0]
    bucket_hot = buckets[None, :] == jnp.arange(bucket_count, dtype=jnp.int32)[:, None]
    offset_values = lax.dot_general(
        table,
        bucket_hot.astype(jnp.bfloat16),
        (((0,), (0,)), ((), ())),
        preferred_element_type=jnp.float32,
    )
    skew = make_skew(jnp.pad(offset_values, ((0, 0), (0, 1))))

    every_float = every_token.astype(jnp.float32)
    tokens_f = every_float[:token_count]
    normed_one, every_inverse = rms_forward(every_float, gain_first)
    inverse_one = every_inverse[:token_count]
    hidden_one = normed_one.astype(jnp.bfloat16)
    queries = jnp.dot(
        hidden_one[:token_count], weight_joint[:, :model_width], preferred_element_type=jnp.float32
    ).astype(jnp.bfloat16) * jnp.bfloat16(SCORE_SCALE)
    key_values = jnp.dot(
        hidden_one, weight_joint[:, model_width:], preferred_element_type=jnp.float32
    ).astype(jnp.bfloat16)
    bases = layout.bases(token_count)
    attended, logsum = attend_forward(bases, queries, key_values, skew)
    attended_low = attended.astype(jnp.bfloat16)
    residual = tokens_f + jnp.dot(attended_low, weight_out, preferred_element_type=jnp.float32)
    normed_two, inverse_two = rms_forward(residual, gain_second)
    hidden_two = normed_two.astype(jnp.bfloat16)

    logits = jnp.dot(hidden_two, weight_router, preferred_element_type=jnp.float32)
    router_prob = jax.nn.softmax(logits, axis=-1)
    is_choice = chosen[:, None] == jnp.arange(expert_count, dtype=jnp.int32)
    choice_hot = is_choice.astype(jnp.float32)
    picked = jnp.sum(router_prob * choice_hot, axis=-1)
    gate_value = kept.astype(jnp.float32) * picked
    most_rows = max(2, (5 * block_len + 4 * expert_count - 1) // (4 * expert_count))
    capacity = seq_count * most_rows
    place = jnp.arange(token_count, dtype=jnp.int32)
    earlier = (place[:, None] >= place[None, :]) & (
        place[:, None] // block_len == place[None, :] // block_len
    )
    running = jnp.dot(
        earlier.astype(jnp.bfloat16),
        is_choice.astype(jnp.bfloat16),
        preferred_element_type=jnp.float32,
    )
    slot_rank = (jnp.sum(running * choice_hot, axis=-1) - 1.0).astype(jnp.int32)
    token_slot = chosen * capacity + place // block_len * most_rows + slot_rank
    slot_hot = (
        (token_slot[:, None] == jnp.arange(expert_count * capacity, dtype=jnp.int32))
        & (kept[:, None] > 0)
    ).astype(jnp.bfloat16)

    def to_experts(row_data):
        sent = lax.dot_general(
            slot_hot, row_data, (((0,), (0,)), ((), ())), preferred_element_type=jnp.float32
        ).astype(jnp.bfloat16)
        arrived = lax.all_to_all(
            sent.reshape(shards, -1, model_width), "exp", split_axis=0, concat_axis=0, tiled=True
        ).reshape(-1, model_width)
        return jnp.concatenate([arrived, layout.swap(arrived, 1)], axis=0)

    def from_experts(partial):
        own_count = partial.shape[0] // 2
        other = layout.swap(partial[own_count:].astype(jnp.bfloat16), 1)
        summed = (partial[:own_count] + other.astype(jnp.float32)).astype(jnp.bfloat16)
        returned = lax.all_to_all(
            summed.reshape(shards, -1, model_width), "exp", split_axis=0, concat_axis=0, tiled=True
        )
        return jnp.dot(
            slot_hot, returned.reshape(-1, model_width), preferred_element_type=jnp.float32
        )

    rows_in = to_experts(hidden_two)
    grad_top = grad_out_low.astype(jnp.float32)
    grad_result = to_experts((gate_value[:, None] * grad_top).astype(jnp.bfloat16))

    acted, gelu_backs = [], []
    produced = 0.0
    for matrix_up, matrix_down in zip(ups, downs):
        before = jnp.dot(rows_in, matrix_up, preferred_element_type=jnp.float32)
        activated, gelu_back = jax.vjp(jax.nn.gelu, before)
        acted.append(activated.astype(jnp.bfloat16))
        gelu_backs.append(gelu_back)
        produced = produced + jnp.dot(acted[-1], matrix_down, preferred_element_type=jnp.float32)
    expert_rows = from_experts(produced)

    grad_inputs = 0.0
    grad_ups, grad_downs = [], []
    for part, (matrix_up, matrix_down) in enumerate(zip(ups, downs)):
        grad_acted = lax.dot_general(
            grad_result, matrix_down, (((1,), (1,)), ((), ())), preferred_element_type=jnp.float32
        )
        grad_before = gelu_backs[part](grad_acted)[0].astype(jnp.bfloat16)
        grad_inputs = grad_inputs + lax.dot_general(
            grad_before, matrix_up, (((1,), (1,)), ((), ())), preferred_element_type=jnp.float32
        )
        grad_ups.append(
            lax.dot_general(
                rows_in, grad_before, (((0,), (0,)), ((), ())), preferred_element_type=jnp.float32
            )
        )
        grad_downs.append(
            lax.dot_general(
                acted[part], grad_result, (((0,), (0,)), ((), ())), preferred_element_type=jnp.float32
            )
        )
    grad_back = from_experts(grad_inputs)

    def own_slice(parts):
        total = parts[0]
        for part, step in zip(parts[1:], list(distances)[1:]):
            total = total + layout.swap(part.astype(jnp.bfloat16), step).astype(jnp.float32)
        return total[None]

    grad_expert_up = own_slice(grad_ups)
    grad_expert_down = own_slice(grad_downs)

    combined = residual + gate_value[:, None] * expert_rows
    layer_out = layout.return_blocks(combined.astype(jnp.bfloat16))

    grad_picked = jnp.sum(grad_top * expert_rows, axis=-1)
    grad_logits = (picked[:, None] * (choice_hot - router_prob) * grad_picked[:, None]).astype(
        jnp.bfloat16
    )
    grad_router = lax.dot_general(
        hidden_two, grad_logits, (((0,), (0,)), ((), ())), preferred_element_type=jnp.float32
    )
    grad_hidden_two = grad_back + lax.dot_general(
        grad_logits, weight_router, (((1,), (1,)), ((), ())), preferred_element_type=jnp.float32
    )
    grad_residual, grad_gain_two = rms_backward(residual, inverse_two, gain_second, grad_hidden_two)
    grad_residual = grad_residual + grad_top
    grad_mixed = grad_residual.astype(jnp.bfloat16)
    grad_weight_out = lax.dot_general(
        attended_low, grad_mixed, (((0,), (0,)), ((), ())), preferred_element_type=jnp.float32
    )
    grad_attended = lax.dot_general(
        grad_mixed, weight_out, (((1,), (1,)), ((), ())), preferred_element_type=jnp.float32
    ).astype(jnp.bfloat16)
    grad_q, grad_k, grad_v, grad_off = attend_backward(
        bases, queries, grad_attended, attended, key_values, skew, logsum
    )

    def back_through(grad_part, first_column):
        return lax.dot_general(
            grad_part,
            weight_joint[:, first_column : first_column + model_width],
            (((1,), (1,)), ((), ())),
            preferred_element_type=jnp.float32,
        )

    grad_hidden_one = layout.sum_rows(
        back_through(grad_k, model_width) + back_through(grad_v, 2 * model_width)
    ) + back_through(grad_q, 0)
    grad_input_norm, grad_gain_one = rms_backward(
        tokens_f, inverse_one, gain_first, grad_hidden_one
    )
    grad_tokens = layout.return_blocks((grad_input_norm + grad_residual).astype(jnp.bfloat16)).astype(
        jnp.float32
    )
    joint_parts = [
        lax.dot_general(
            hidden_one[: part.shape[0]], part, (((0,), (0,)), ((), ())), preferred_element_type=jnp.float32
        ).astype(jnp.bfloat16)
        for part in (grad_q, grad_k, grad_v)
    ]
    grad_table = jnp.dot(
        bucket_hot.astype(jnp.float32),
        grad_off.reshape(head_count, -1)[:, :offset_count].T,
        precision=HIGHEST,
    )

    def scatter(part):
        return lax.psum_scatter(part.astype(jnp.bfloat16), "exp", scatter_dimension=0, tiled=True)

    small_grads = [grad_gain_one, grad_gain_two, grad_router, grad_table]
    small_sum = scatter(
        jnp.concatenate([part.reshape(shards, -1) for part in small_grads], axis=1)
    )
    out_sum = scatter(grad_weight_out)
    joint_sum = scatter(jnp.concatenate(joint_parts, axis=1))
    small_sum, out_sum, joint_sum = lax.psum((small_sum, out_sum, joint_sum), "ctx")
    small_sum = small_sum[0].astype(jnp.float32)
    sum_gain_one, sum_gain_two, sum_router, sum_table = jnp.split(small_sum, small_cuts)
    return (
        layer_out,
        grad_tokens,
        sum_gain_one,
        joint_sum.astype(jnp.float32),
        out_sum.astype(jnp.float32),
        sum_table.reshape(bias_table.shape),
        sum_gain_two,
        sum_router.reshape(router_weight.shape),
        grad_expert_up,
        grad_expert_down,
    )


def solution(mesh):
    in_specs = (
        P("exp", "ctx", None),
        P("exp"),
        P("exp", None),
        P("exp", None),
        P("exp", None),
        P("exp"),
        P("exp", None),
        P("exp", None, "ctx"),
        P("exp", "ctx", None),
        P("exp", "ctx", None),
        P("exp", "ctx"),
        P(),
        P("exp", "ctx", None),
    )
    out_specs = (
        P("exp", "ctx", None),
        P("exp", "ctx", None),
        P("exp"),
        P("exp", None),
        P("exp", None),
        P("exp", None),
        P("exp"),
        P("exp", None),
        P("exp", None, "ctx"),
        P("exp", "ctx", None),
    )
    return jax.shard_map(
        per_device, mesh=mesh, in_specs=in_specs, out_specs=out_specs, check_vma=False
    )
```

time: 1460 us -> 595 us (0.41)
  local copies, waits for them, and re-layouts: 599 us -> 24.4 us
  waiting for transfers between devices: 493 us -> 269 us
  matrix products: 181 us -> 88.6 us
  Pallas kernels: 0 us -> 55.8 us
  other arithmetic: 48 us -> 20.6 us
  starting transfers between devices: 17.2 us -> 43.2 us
  loops' own time: 22.5 us -> 0 us
    reduce_scatter x5 -> x1, waiting for transfers between devices: 310 us -> 0.01 us  [scatter(): lax.psum_scatter(part.astype(jnp.bfloat16), 'exp', scatter_dimension=0, t...]
    reshape x17 -> x10, local copies, waits for them, and re-layouts: 298 us -> 1.18 us  [the longest x4 0.51 us: per_device(): part.reshape(shards, -1)]
    ppermute x0 -> x20, waiting for transfers between devices: none -> 196 us  [the longest x8 188 us: swap(): return lax.ppermute(rows, 'ctx', pairs)]
    slice x27 -> x4, local copies, waits for them, and re-layouts: 166 us -> 2.24 us  [the longest x2 1.28 us: from_experts(): other = layout.swap(partial[own_count:].astype(jnp.bfloat16), 1)]
    all_gather x5 -> x2, waiting for transfers between devices: 120 us -> 0.04 us  [the longest x1 0.02 us: per_device(): weight_joint = lax.all_gather(joint_projection, 'exp', axis=0, tiled=True)]
    dot_general x31 -> x32, matrix products: 179 us -> 85.4 us  [the longest x2 11.2 us: per_device(): lax.dot_general(grad_result, matrix_down, (((1,), (1,)), ((), ())), prefe...]
    pallas_call x0 -> x3, Pallas kernels: none -> 55.8 us  [the longest x1 27.7 us: attend_backward(): pl.pallas_call(functools.partial(backward_kernel, chunk=chunk), grid_spec...]
    pad x4 -> x1, local copies, waits for them, and re-layouts: 38.1 us -> 0.02 us  [per_device(): skew = make_skew(jnp.pad(offset_values, ((0, 0), (0, 1))))]
  transfers between devices with their start and end apart: 16 -> 29, of which waited for: 10 -> 13; matrix products, arithmetic and copies ran while one was open for 29% -> 19% of each run, Pallas kernels for 0% -> 5%
where the time goes in v1:
time: 595 us; the launch traced here: 585 us
  waiting for transfers between devices  269 us (45%)
  matrix products  88.6 us (15%)
  blocking collectives  67.7 us (11%)
  Pallas kernels  55.8 us (9%)
  starting transfers between devices  43.2 us (7%)
  local copies, waits for them, and re-layouts  24.4 us (4%)
  other arithmetic  20.6 us (3%)
  between operations  15.7 us (3%)
    ppermute x8, waiting for transfers between devices, swap(): return lax.ppermute(rows, 'ctx', pairs)  188 us
    unnamed x2, blocking collectives  58.3 us
    psum x1, waiting for transfers between devices, per_device(): lax.psum((small_sum, out_sum, joint_sum), 'ctx')  38.4 us
    pallas_call x1, Pallas kernels, attend_backward(): pl.pallas_call(functools.partial(backward_kernel, chunk=chunk), grid_spec...  27.7 us
    all_to_all x2, waiting for transfers between devices, to_experts(): lax.all_to_all(sent.reshape(shards, -1, model_width), 'exp', split_axis=0...  24.6 us
    pallas_call x1, Pallas kernels, attend_forward(): pl.pallas_call(functools.partial(forward_kernel, chunk=chunk), grid_spec=...  20.7 us
    unnamed x91, local copies, waits for them, and re-layouts  15.6 us
    ppermute x6, starting transfers between devices, gather_blocks(): lax.ppermute(lax.dynamic_index_in_dim(blocks, (turn + self.ctx) % 2, 0, k...  12.3 us
  transfers between devices with their start and end apart: 29, of which 13 were waited for; matrix products, arithmetic and copies ran while one was open for 19% of the time, Pallas kernels for 5%

profile of v1, /device:TPU:0, one launch (start us, length us, event | category | flops | bytes accessed | tf_op | source)
XLA Modules:
  0.0 585.2 jit_solution(17353170340692931637)
XLA Ops:
  21.9 30.0 %all-reduce.1 = bf16[8064]{0:T(1024)(128)(2,1)S(1)} all-reduce(bf16[8064]{0:T(1024)(128)(2,1)S(1)} %dynamic-update-slice), channel_id=2, replica_groups=mesh['ctx'=4,'exp'=8] {'exp'}, use_global_device_ids=true, to_apply=%add.1 | all-reduce | flops 8064 | bytes 32256
  53.0 7.4 %skew_bias.1.skew_ref = bf16[12,1920,128]{2,1,0:T(8,128)(2,1)} custom-call(f32[12,1,2048]{2,1,0:T(1,128)S(1)} %reshape.420.offset_ref), custom_call_target="tpu_custom_call" | custom-call | tf_op jit(solution)/shard_map/skew_bias/pallas_call | solution.py:43
  76.0 20.7 %attend_forward.1 = (f32[512,768]{1,0:T(8,128)S(1)}, f32[6,2,512]{2,1,0:T(2,128)S(1)}) custom-call(s32[2]{0:T(128)S(1)} %pad_add_fusion.1.base_ref, bf16[512,768]{1,0:T(8,128)(2,1)S(1)} %fusion.26.q_ref, bf16[1024,1536]{1,0:T(8,128)(2,1)} %convolution_convert_fusion.k_ref.v_ref, bf16[1024,1536]{1,0:T(8,128)(2,1)} %convolution_convert_fusion.k_ref.v_ref, ...), custom_call_target="tpu_custom_call" | custom-call | tf_op jit(solution)/shard_map/attend_forward/pallas_call | solution.py:107
  107.8 13.1 %all-to-all-done = bf16[8,80,768]{2,1,0:T(8,128)(2,1)} async-done(((bf16[8,80,768]{2,1,0:T(8,128)(2,1)}), bf16[8,80,768]{2,1,0:T(8,128)(2,1)}, u32[]{:S(2)}, u32[]{:S(2)}) %all-to-all-start) | async-done | bytes 983072 | tf_op jit(solution)/shard_map/all_to_all | solution.py:447
  130.2 11.5 %all-to-all-done.2 = bf16[8,80,768]{2,1,0:T(8,128)(2,1)} async-done(((bf16[8,80,768]{2,1,0:T(8,128)(2,1)}), bf16[8,80,768]{2,1,0:T(8,128)(2,1)}, u32[]{:S(2)}, u32[]{:S(2)}) %all-to-all-start.2) | async-done | bytes 983072 | tf_op jit(solution)/shard_map/all_to_all | solution.py:447
  143.8 10.4 %collective-permute-done.5 = bf16[640,768]{1,0:T(8,128)(2,1)} collective-permute-done((bf16[640,768]{1,0:T(8,128)(2,1)}, bf16[640,768]{1,0:T(8,128)(2,1)}, u32[]{:S(2)}, u32[]{:S(2)}) %collective-permute-start.5) | collective-permute-done | bytes 983072 | tf_op jit(solution)/shard_map/ppermute | solution.py:339
  160.2 47.7 %collective-permute-done.6 = bf16[768,768]{1,0:T(8,128)(2,1)} collective-permute-done((bf16[768,768]{1,0:T(8,128)(2,1)}, bf16[768,768]{1,0:T(8,128)(2,1)}, u32[]{:S(2)}, u32[]{:S(2)}) %collective-permute-start.6) | collective-permute-done | bytes 1179680 | tf_op jit(solution)/shard_map/ppermute | solution.py:339
  211.5 21.1 %collective-permute-done.7 = bf16[768,768]{1,0:T(8,128)(2,1)} collective-permute-done((bf16[768,768]{1,0:T(8,128)(2,1)}, bf16[768,768]{1,0:T(8,128)(2,1)}, u32[]{:S(2)}, u32[]{:S(2)}) %collective-permute-start.7) | collective-permute-done | bytes 1179680 | tf_op jit(solution)/shard_map/ppermute | solution.py:339
  236.6 5.5 fusion.13
  242.1 5.7 fusion.6
  255.8 5.4 collective-permute-done.8
  266.6 14.3 %collective-permute-done.14 = bf16[640,768]{1,0:T(8,128)(2,1)} collective-permute-done((bf16[640,768]{1,0:T(8,128)(2,1)}, bf16[640,768]{1,0:T(8,128)(2,1)}, u32[]{:S(2)}, u32[]{:S(2)}) %collective-permute-start.14) | collective-permute-done | bytes 983072 | tf_op jit(solution)/shard_map/ppermute | solution.py:339
  293.0 9.8 %all-to-all-done.3 = bf16[8,80,768]{2,1,0:T(8,128)(2,1)} async-done(((bf16[8,80,768]{2,1,0:T(8,128)(2,1)}), bf16[8,80,768]{2,1,0:T(8,128)(2,1)}, u32[]{:S(2)}, u32[]{:S(2)}) %all-to-all-start.3) | async-done | bytes 983072 | tf_op jit(solution)/shard_map/all_to_all | solution.py:456
  308.3 27.7 %attend_backward.1 = (bf16[512,768]{1,0:T(8,128)(2,1)S(1)}, bf16[1024,768]{1,0:T(8,128)(2,1)S(1)}, bf16[1024,768]{1,0:T(8,128)(2,1)}, f32[6,2,2048]{2,1,0:T(2,128)S(1)}) custom-call(s32[2]{0:T(128)S(1)} %pad_add_fusion.1.base_ref, bf16[512,768]{1,0:T(8,128)(2,1)S(1)} %fusion.26.q_ref, bf16[512,768]{1,0:T(8,128)(2,1)S(1)} %convolution_convert_fusion.9.do_ref, ...), custom_call_target="tpu_custom_call" | custom-call | tf_op jit(solution)/shard_map/attend_backward/pallas_call | solution.py:205
  342.3 5.8 copy.37
  348.3 5.0 convolution_convert_fusion.2
  360.7 68.9 %collective-permute-done.18 = bf16[768,768]{1,0:T(8,128)(2,1)S(1)} collective-permute-done((bf16[768,768]{1,0:T(8,128)(2,1)}, bf16[768,768]{1,0:T(8,128)(2,1)S(1)}, u32[]{:S(2)}, u32[]{:S(2)}) %collective-permute-start.18) | collective-permute-done | bytes 1179680 | tf_op jit(solution)/shard_map/ppermute | solution.py:339
  429.6 5.3 add_bitcast_fusion.1
  434.9 20.0 %collective-permute-done.19 = bf16[768,768]{1,0:T(8,128)(2,1)} collective-permute-done((bf16[768,768]{1,0:T(8,128)(2,1)}, bf16[768,768]{1,0:T(8,128)(2,1)}, u32[]{:S(2)}, u32[]{:S(2)}) %collective-permute-start.19) | collective-permute-done | bytes 1179680 | tf_op jit(solution)/shard_map/ppermute | solution.py:339
  454.9 5.1 add_bitcast_fusion
  480.0 28.3 %all-reduce.2 = bf16[8,1008]{1,0:T(8,128)(2,1)S(1)} all-reduce(bf16[8,1008]{1,0:T(8,128)(2,1)S(1)} %pad_maximum_fusion.8), channel_id=3, replica_groups=mesh['ctx'=4,'exp'=8] {'exp'}, use_global_device_ids=true, to_apply=%region_11.12.clone | all-reduce | flops 8064 | bytes 32256
  509.0 9.5 %psum.21 = bf16[1,1008]{1,0:T(2,128)(2,1)S(1)} all-reduce(bf16[1,1008]{1,0:T(2,128)(2,1)S(1)} %constant_dynamic-slice_fusion.2), channel_id=1, replica_groups=mesh['ctx'=4,'exp'=8] {'ctx'}, use_global_device_ids=true, to_apply=%region_12.13 | all-reduce | flops 1008 | bytes 4032 | tf_op jit(solution)/shard_map/psum | solution.py:572
  526.8 6.0 %collective-permute-done.17 = bf16[256,768]{1,0:T(8,128)(2,1)S(1)} collective-permute-done((bf16[256,768]{1,0:T(8,128)(2,1)S(1)}, bf16[256,768]{1,0:T(8,128)(2,1)S(1)}, u32[]{:S(2)}, u32[]{:S(2)}) %collective-permute-start.17) | collective-permute-done | bytes 393248 | tf_op jit(solution)/shard_map/ppermute | solution.py:305
  536.2 38.4 %all-reduce.6.cloned.1.call-done = (bf16[96,2304]{0,1:T(8,128)(2,1)}, bf16[96,768]{1,0:T(8,128)(2,1)}) async-done(((bf16[96,2304]{0,1:T(8,128)(2,1)}, bf16[96,768]{1,0:T(8,128)(2,1)}), (bf16[96,2304]{0,1:T(8,128)(2,1)}, bf16[96,768]{1,0:T(8,128)(2,1)})) %all-reduce.6.cloned.1.call-update) | async-done | bytes 589840 | tf_op jit(solution)/shard_map/psum | solution.py:572
  (235 shorter events, 147.0 us)
Async XLA Ops:
  7.2 61.8 %all-gather.4.cloned.1.call-start = ((), (), s32[]{:S(2)}) async-start(), calls=%async_computation.6 | async-start | bytes 3981312 | tf_op jit(solution)/shard_map/all_gather | solution.py:376
  8.0 88.7 %all-gather.6.cloned.1.call-start = ((), (), s32[]{:S(2)}) async-start(), calls=%async_computation.7 | async-start | bytes 1327104 | tf_op jit(solution)/shard_map/all_gather | solution.py:377
  8.8 55.2 %collective-permute-start.4 = (s32[256]{0:T(256)S(1)}, s32[256]{0:T(256)S(1)}, u32[]{:S(2)}, u32[]{:S(2)}) collective-permute-start(s32[256]{0:T(256)S(1)} %bitcast.88), channel_id=1, source_target_pairs={{0,8},{1,24},{2,10},{3,26},{4,12},{5,28},{6,14},{7,30},{8,0},{9,16... | collective-permute-start | bytes 3080 | tf_op jit(solution)/shard_map/ppermute | solution.py:291
  11.9 52.1 %collective-permute-start.3 = (s32[256]{0:T(256)S(1)}, s32[256]{0:T(256)S(1)}, u32[]{:S(2)}, u32[]{:S(2)}) collective-permute-start(s32[256]{0:T(256)S(1)} %bitcast.87), channel_id=1, source_target_pairs={{0,0},{1,16},{2,2},{3,18},{4,4},{5,20},{6,6},{7,22},{8,8},{9,24},{... | collective-permute-start | bytes 3080 | tf_op jit(solution)/shard_map/ppermute | solution.py:291
  13.7 46.8 %collective-permute-start = (bf16[256,768]{1,0:T(8,128)(2,1)S(1)}, bf16[256,768]{1,0:T(8,128)(2,1)S(1)}, u32[]{:S(2)}, u32[]{:S(2)}) collective-permute-start(bf16[256,768]{1,0:T(8,128)(2,1)S(1)} %get-tuple-element.80), channel_id=1, source_target_pairs={{0,0},{1,16},{2,2},{3,18},{4,4},{5,20},{6,6},{7,22},{8,8},{9,24},{... | collective-permute-start | bytes 1179656 | tf_op jit(solution)/shard_map/ppermute | solution.py:291
  14.4 49.4 %collective-permute-start.1 = (bf16[256,768]{1,0:T(8,128)(2,1)S(1)}, bf16[256,768]{1,0:T(8,128)(2,1)S(1)}, u32[]{:S(2)}, u32[]{:S(2)}) collective-permute-start(bf16[256,768]{1,0:T(8,128)(2,1)S(1)} %get-tuple-element.81), channel_id=1, source_target_pairs={{0,8},{1,24},{2,10},{3,26},{4,12},{5,28},{6,14},{7,30},{8,0},{9,16... | collective-permute-start | bytes 1179656 | tf_op jit(solution)/shard_map/ppermute | solution.py:291
  15.4 90.8 %collective-permute-start.11 = (bf16[256,768]{1,0:T(8,128)(2,1)}, bf16[256,768]{1,0:T(8,128)(2,1)}, u32[]{:S(2)}, u32[]{:S(2)}) collective-permute-start(bf16[256,768]{1,0:T(8,128)(2,1)} %get-tuple-element.72), channel_id=1, source_target_pairs={{0,0},{1,16},{2,2},{3,18},{4,4},{5,20},{6,6},{7,22},{8,8},{9,24},{... | collective-permute-start | bytes 1179656 | tf_op jit(solution)/shard_map/ppermute | solution.py:291
  60.5 45.7 %collective-permute-start.12 = (bf16[256,768]{1,0:T(8,128)(2,1)}, bf16[256,768]{1,0:T(8,128)(2,1)}, u32[]{:S(2)}, u32[]{:S(2)}) collective-permute-start(bf16[256,768]{1,0:T(8,128)(2,1)} %get-tuple-element.73), channel_id=1, source_target_pairs={{0,8},{1,24},{2,10},{3,26},{4,12},{5,28},{6,14},{7,30},{8,0},{9,16... | collective-permute-start | bytes 1179656 | tf_op jit(solution)/shard_map/ppermute | solution.py:291
  101.9 19.0 %all-to-all-start = ((bf16[8,80,768]{2,1,0:T(8,128)(2,1)}), bf16[8,80,768]{2,1,0:T(8,128)(2,1)}, u32[]{:S(2)}, u32[]{:S(2)}) async-start(bf16[8,80,768]{2,1,0:T(8,128)(2,1)} %bitcast.8), calls=%async_computation | async-start | bytes 1966080 | tf_op jit(solution)/shard_map/all_to_all | solution.py:447
  120.9 33.3 %collective-permute-start.5 = (bf16[640,768]{1,0:T(8,128)(2,1)}, bf16[640,768]{1,0:T(8,128)(2,1)}, u32[]{:S(2)}, u32[]{:S(2)}) collective-permute-start(bf16[640,768]{1,0:T(8,128)(2,1)} %bitcast.9), channel_id=1, source_target_pairs={{0,8},{8,0},{16,24},{24,16},{1,9},{9,1},{17,25},{25,17},{2,10},{10... | collective-permute-start | bytes 2949128 | tf_op jit(solution)/shard_map/ppermute | solution.py:339
  127.2 80.7 %collective-permute-start.6 = (bf16[768,768]{1,0:T(8,128)(2,1)}, bf16[768,768]{1,0:T(8,128)(2,1)}, u32[]{:S(2)}, u32[]{:S(2)}) collective-permute-start(bf16[768,768]{1,0:T(8,128)(2,1)} %bitcast.92), channel_id=1, source_target_pairs={{0,16},{8,24},{16,0},{24,8},{1,17},{9,25},{17,1},{25,9},{2,18},{10... | collective-permute-start | bytes 3538952 | tf_op jit(solution)/shard_map/ppermute | solution.py:339
  127.3 105.3 %collective-permute-start.7 = (bf16[768,768]{1,0:T(8,128)(2,1)}, bf16[768,768]{1,0:T(8,128)(2,1)}, u32[]{:S(2)}, u32[]{:S(2)}) collective-permute-start(bf16[768,768]{1,0:T(8,128)(2,1)} %bitcast.89), channel_id=1, source_target_pairs={{0,16},{8,24},{16,0},{24,8},{1,17},{9,25},{17,1},{25,9},{2,18},{10... | collective-permute-start | bytes 3538952 | tf_op jit(solution)/shard_map/ppermute | solution.py:339
  141.8 94.8 %collective-permute-start.13 = (bf16[640,768]{1,0:T(8,128)(2,1)}, bf16[640,768]{1,0:T(8,128)(2,1)S(1)}, u32[]{:S(2)}, u32[]{:S(2)}) collective-permute-start(bf16[640,768]{1,0:T(8,128)(2,1)} %bitcast.22), channel_id=1, source_target_pairs={{0,8},{8,0},{16,24},{24,16},{1,9},{9,1},{17,25},{25,17},{2,10},{10... | collective-permute-start | bytes 2949128 | tf_op jit(solution)/shard_map/ppermute | solution.py:339
  236.5 24.7 %collective-permute-start.8 = (bf16[640,768]{1,0:T(8,128)(2,1)S(1)}, bf16[640,768]{1,0:T(8,128)(2,1)S(1)}, u32[]{:S(2)}, u32[]{:S(2)}) collective-permute-start(bf16[640,768]{1,0:T(8,128)(2,1)S(1)} %slice.124), channel_id=1, source_target_pairs={{0,8},{8,0},{16,24},{24,16},{1,9},{9,1},{17,25},{25,17},{2,10},{10... | collective-permute-start | bytes 2949128 | tf_op jit(solution)/shard_map/ppermute | solution.py:339
  253.8 27.1 %collective-permute-start.14 = (bf16[640,768]{1,0:T(8,128)(2,1)}, bf16[640,768]{1,0:T(8,128)(2,1)}, u32[]{:S(2)}, u32[]{:S(2)}) collective-permute-start(bf16[640,768]{1,0:T(8,128)(2,1)} %slice.123), channel_id=1, source_target_pairs={{0,8},{8,0},{16,24},{24,16},{1,9},{9,1},{17,25},{25,17},{2,10},{10... | collective-permute-start | bytes 2949128 | tf_op jit(solution)/shard_map/ppermute | solution.py:339
  262.4 21.5 %all-to-all-start.1 = ((bf16[8,80,768]{2,1,0:T(8,128)(2,1)}), bf16[8,80,768]{2,1,0:T(8,128)(2,1)}, u32[]{:S(2)}, u32[]{:S(2)}) async-start(bf16[8,80,768]{2,1,0:T(8,128)(2,1)} %bitcast.12), calls=%async_computation.1 | async-start | bytes 1966080 | tf_op jit(solution)/shard_map/all_to_all | solution.py:456
  283.9 19.0 %all-to-all-start.3 = ((bf16[8,80,768]{2,1,0:T(8,128)(2,1)}), bf16[8,80,768]{2,1,0:T(8,128)(2,1)}, u32[]{:S(2)}, u32[]{:S(2)}) async-start(bf16[8,80,768]{2,1,0:T(8,128)(2,1)} %bitcast.23), calls=%async_computation.3 | async-start | bytes 1966080 | tf_op jit(solution)/shard_map/all_to_all | solution.py:456
  288.1 235.0 %reduce-scatter.7.cloned.1.call-start = ((), (), s32[]{:S(2)}) async-start(), calls=%async_computation.9 | async-start | bytes 3981312
  348.1 177.2 %reduce-scatter.5.cloned.1.call-start = ((), (), s32[]{:S(2)}) async-start(), calls=%async_computation.8 | async-start | bytes 1327104 | tf_op jit(solution)/shard_map/reduce_scatter | solution.py:564
  353.4 76.2 %collective-permute-start.18 = (bf16[768,768]{1,0:T(8,128)(2,1)}, bf16[768,768]{1,0:T(8,128)(2,1)S(1)}, u32[]{:S(2)}, u32[]{:S(2)}) collective-permute-start(bf16[768,768]{1,0:T(8,128)(2,1)} %convolution_convert_fusion.2), channel_id=1, source_target_pairs={{0,16},{8,24},{16,0},{24,8},{1,17},{9,25},{17,1},{25,9},{2,18},{10... | collective-permute-start | bytes 3538952 | tf_op jit(solution)/shard_map/ppermute | solution.py:339
  358.6 96.3 %collective-permute-start.19 = (bf16[768,768]{1,0:T(8,128)(2,1)}, bf16[768,768]{1,0:T(8,128)(2,1)}, u32[]{:S(2)}, u32[]{:S(2)}) collective-permute-start(bf16[768,768]{1,0:T(8,128)(2,1)} %convolution_convert_fusion.1), channel_id=1, source_target_pairs={{0,16},{8,24},{16,0},{24,8},{1,17},{9,25},{17,1},{25,9},{2,18},{10... | collective-permute-start | bytes 3538952 | tf_op jit(solution)/shard_map/ppermute | solution.py:339
  471.1 103.6 %all-reduce.6.cloned.1.call-start = ((), (), s32[]{:S(2)}) async-start(), calls=%async_computation.10 | async-start | bytes 1474560 | tf_op jit(solution)/shard_map/psum | solution.py:572
  473.5 53.3 %collective-permute-start.9 = (bf16[256,768]{1,0:T(8,128)(2,1)S(1)}, bf16[256,768]{1,0:T(8,128)(2,1)}, u32[]{:S(2)}, u32[]{:S(2)}) collective-permute-start(bf16[256,768]{1,0:T(8,128)(2,1)S(1)} %get-tuple-element.76), channel_id=1, source_target_pairs={{0,0},{16,1},{2,2},{18,3},{4,4},{20,5},{6,6},{22,7},{8,8},{24,9},{... | collective-permute-start | bytes 1179656 | tf_op jit(solution)/shard_map/ppermute | solution.py:305
  475.1 51.7 %collective-permute-start.10 = (bf16[256,768]{1,0:T(8,128)(2,1)S(1)}, bf16[256,768]{1,0:T(8,128)(2,1)}, u32[]{:S(2)}, u32[]{:S(2)}) collective-permute-start(bf16[256,768]{1,0:T(8,128)(2,1)S(1)} %get-tuple-element.77), channel_id=1, source_target_pairs={{8,0},{24,1},{10,2},{26,3},{12,4},{28,5},{14,6},{30,7},{0,8},{16,9... | collective-permute-start | bytes 1179656 | tf_op jit(solution)/shard_map/ppermute | solution.py:305
  (46 other events, 1021.5 us)
Sparse Core Ops, SparseCore 0:
  10.0 36.8 all-gather.3
  48.7 24.1 all-gather.5
  348.2 45.8 reduce-scatter.6
  471.2 37.7 reduce-scatter.4
  525.4 49.1 all-reduce.5
